TPU v7x, 32 devices: a whole 2x2x4 slice. The times are simulated.
32 devices in a mesh: rows: 4 (over y, core), cols: 8 (over z, x).
Axes of the slice: x: 2, y: 2, z: 4, core: 2. Of those that a mesh axis runs over, the one named last changes fastest.
Arguments:
- displacement: float32 [2048, 288], P(('rows', 'cols')), may hold values from -6 to 6
- positions: float32 [2048, 288], P(('rows', 'cols')), as said below
- cluster_basis: bfloat16 [2048, 288, 64], P(('rows', 'cols')), may hold values from -0.375 to 0.375
- near_pairs: int32 [8192, 2], P(('rows', 'cols')), may hold values from 0 to 67, as said below
- near_count: int32 [32], P(('rows', 'cols')), may hold values from 64 to 256, as said below
- far_pairs: int32 [32768, 2], P(('rows', 'cols')), may hold values from 0 to 511, as said below
- far_count: int32 [32], P(('rows', 'cols')), may hold values from 256 to 1024, as said below
- far_blocks: bfloat16 [32768, 64, 64], P(('rows', 'cols')), may hold values from -0.75 to 0.75
- intact: int32 [2048, 96], P(('rows', 'cols')), may hold values 0 or 1
- stiffness: float32 [2048, 96], P(('rows', 'cols')), may hold values from 0.5 to 2
Outputs:
- net_traction: float32 [2048, 288], P(('rows', 'cols'))
- damage: float32 [2048, 96], P(('rows', 'cols'))
Inputs may be any that keep to these rules, and one draw needn't show every extreme that they name: `positions`: centroids of the elements of each cluster. `near_pairs`: column 0 is a cluster of the device's own 64; column 1 counts from 2 clusters before the device's first cluster and names a cluster at most 2 away from the target in the cluster order. Dead slots hold valid entries too. `near_count`: loads differ from device to device. `far_pairs`: column 0 is a target cluster of the device's index along rows (0 to 511); column 1 a source cluster of its index along cols (0 to 255), numbered through the devices of that column in the order of rows. Dead slots hold valid entries too. `far_count`: loads differ from device to device.
All inputs are finite; a program needn't handle non-finite values. No bound on the sum of `intact` on one device may be relied on, other than what follows from the above.
Results may differ from a plain program's by a relative error of at most 0.0014.
Values may be sent and summed in bfloat16 or wider, within the bound.
No kernel may reach another device: no remote copies, remote signals or barrier semaphores. Data moves between devices by JAX's collectives and lax.ppermute only.
A program may use at most 128 MiB of HBM per device.

v0:
```python
import jax
import jax.numpy as jnp
from jax import lax
from jax.sharding import PartitionSpec as P

HALO = 2


core_square = 0.25
softening = 1.5
pair_group = 32


def with_halo(array, sides, width):
    for axis, dim in sides:
        devices, length = (lax.axis_size(axis), array.shape[dim])
        up = [(i, (i + 1) % devices) for i in range(devices - 1)]
        down = [(j, i) for i, j in up]
        last = lax.slice_in_dim(array, length - width, length, axis=dim)
        leading = lax.slice_in_dim(array, 0, width, axis=dim)
        before = lax.ppermute(last, axis, up)
        after = lax.ppermute(leading, axis, down)
        array = jnp.concatenate([before, array, after], axis=dim)
    return array


def kernel_block(target_pos, source_pos, source_disp):
    offsets = target_pos[:, :, :, None] - source_pos[:, :, None, :]
    distance = jnp.sum(offsets * offsets, axis=1) + core_square
    inverse = lax.rsqrt(distance)
    inverse = inverse * inverse * inverse
    along = jnp.sum(offsets * source_disp[:, :, None, :], axis=1)
    direct = jnp.sum(inverse[:, None, :, :] * source_disp[:, :, None, :], axis=3)
    second = jnp.sum(offsets * (along * inverse / distance)[:, None, :, :], axis=3)
    return direct - 3.0 * second


def local(
    displacement,
    positions,
    cluster_basis,
    near_pairs,
    near_count,
    far_pairs,
    far_count,
    far_blocks,
    intact,
    stiffness,
):
    clusters = displacement.shape[0]
    row_width = displacement.shape[1]
    elems = row_width // 3
    stacked = jnp.stack([displacement, positions])
    extended = with_halo(stacked, ((("rows", "cols"), 1),), HALO)
    ext_disp = extended[0]
    ext_pos = extended[1]
    near_slots = near_pairs.shape[0]
    group_size = min(pair_group, near_slots)

    def near_step(group_index, summed):
        first_slot = group_index * group_size
        chosen = lax.dynamic_slice_in_dim(near_pairs, first_slot, group_size, 0)
        targets = chosen[:, 0]
        sources = chosen[:, 1]
        active = (first_slot + jnp.arange(group_size, dtype=jnp.int32) < near_count[0]).astype(
            jnp.float32
        )
        target_pos = positions[targets].reshape(group_size, 3, elems)
        source_pos = ext_pos[sources].reshape(group_size, 3, elems)
        source_disp = ext_disp[sources].reshape(group_size, 3, elems)
        contrib = kernel_block(target_pos, source_pos, source_disp) * active[:, None, None]
        return summed.at[targets].add(contrib.reshape(group_size, row_width))

    near_sum = lax.fori_loop(
        0, near_slots // group_size, near_step, jnp.zeros((clusters, row_width), jnp.float32)
    )
    disp_bf = displacement.astype(jnp.bfloat16)
    coeff = jnp.einsum("kf,kfr->kr", disp_bf, cluster_basis, preferred_element_type=jnp.float32)
    coeff_bf = coeff.astype(jnp.bfloat16)
    column = lax.all_gather(coeff_bf, "rows", axis=0, tiled=True)
    far_slots = far_pairs.shape[0]
    far_active = (jnp.arange(far_slots, dtype=jnp.int32) < far_count[0]).astype(jnp.float32)
    gathered = column[far_pairs[:, 1]]
    coupled = (
        jnp.einsum("prs,ps->pr", far_blocks, gathered, preferred_element_type=jnp.float32)
        * far_active[:, None]
    )
    row_clusters = clusters * lax.axis_size("cols")
    partial_sum = (
        jnp.zeros((row_clusters, coeff.shape[1]), jnp.float32).at[far_pairs[:, 0]].add(coupled)
    )
    whole = lax.psum(partial_sum.astype(jnp.bfloat16), "cols").astype(jnp.float32)
    owned = lax.dynamic_slice_in_dim(whole, lax.axis_index("cols") * clusters, clusters, 0)
    owned_bf = owned.astype(jnp.bfloat16)
    far_part = jnp.einsum("kfr,kr->kf", cluster_basis, owned_bf, preferred_element_type=jnp.float32)
    traction = near_sum + far_part
    disp3 = displacement.reshape(clusters, 3, elems)
    separation = jnp.sqrt(1.0 + jnp.sum(disp3 * disp3, axis=1))
    softened = 1.0 - jnp.exp(-(separation - 1.0) / softening)
    intact_float = intact.astype(jnp.float32)
    damage = intact_float * softened + (1.0 - intact_float)
    holding = ((1.0 - damage) * stiffness)[:, None, :] * disp3
    net_traction = traction - holding.reshape(clusters, row_width)
    return (net_traction, damage)


def solution(mesh):
    in_specs = (
        P(("rows", "cols"), None),
        P(("rows", "cols"), None),
        P(("rows", "cols"), None, None),
        P(("rows", "cols"), None),
        P(("rows", "cols")),
        P(("rows", "cols"), None),
        P(("rows", "cols")),
        P(("rows", "cols"), None, None),
        P(("rows", "cols"), None),
        P(("rows", "cols"), None),
    )
    out_specs = (P(("rows", "cols"), None), P(("rows", "cols"), None))
    return jax.shard_map(local, mesh=mesh, in_specs=in_specs, out_specs=out_specs, check_vma=False)
```

profile of v0, /device:TPU:0, one launch (start us, length us, event | category | flops | bytes accessed | tf_op | source)
XLA Modules:
  0.0 245.8 jit_solution(5835879457687178342)
XLA Ops:
  10.0 6.1 %collective-permute-start = (f32[2,2,288]{2,1,0:T(2,128)S(1)}, f32[2,2,288]{2,1,0:T(2,128)}, u32[]{:S(2)}, u32[]{:S(2)}) collective-permute-start(f32[2,2,288]{2,1,0:T(2,128)S(1)} %get-tuple-element.155), channel_id=1, source_target_pairs={{0,1},{1,2},{2,3},{3,4},{4,5},{5,6},{6,7},{7,8},{8,9},{9,10},{10,1... | collective-permute-start | bytes 13832 | tf_op jit(solution)/shard_map/ppermute | solution.py:21
  16.1 1.6 convert_bitcast_fusion
  18.5 29.2 %copy.15 = bf16[1024,64,64]{1,2,0:T(8,128)(2,1)} copy(bf16[1024,64,64]{0,2,1:T(8,128)(2,1)} %param.19) | data formatting | bytes 16777216 | tf_op args[7]
  48.9 7.3 %all_gather.3 = bf16[256,64]{1,0:T(8,128)(2,1)S(1)} all-gather(bf16[64,64]{1,0:T(8,128)(2,1)S(1)} %convert_element_type.37), channel_id=1, replica_groups=mesh['rows'=4,'cols'=8] {'rows'}, dimensions={0}, use_global_device_ids=true | all-gather | bytes 40960 | tf_op jit(solution)/shard_map/all_gather | solution.py:80
  56.8 4.3 %gather_fusion.3 = bf16[1024,64]{1,0:T(8,128)(2,1)} fusion(bf16[256,64]{1,0:T(8,128)(2,1)S(1)} %all_gather.3, s32[1024]{0:T(1024)S(1)} %broadcast_clamp_fusion), kind=kCustom, calls=%fused_computation.3 | custom fusion | bytes 266240 | tf_op jit(solution)/shard_map/gather | solution.py:83
  61.1 8.9 %fusion.8 = f32[1024,1,64]{2,1,0:T(1,128)} fusion(bf16[1024,64,64]{1,2,0:T(8,128)(2,1)} %copy.15, bf16[1024,64,1]{1,0,2:T(8,128)(2,1)} %bitcast.40), kind=kOutput, calls=%fused_computation.27 | convolution fusion | flops 8388608 | bytes 8781824 | tf_op jit(solution)/shard_map/prs,ps->pr/dot_general | solution.py:85
  70.0 7.6 %scatter_custom_fusion.1 = f32[512,64]{1,0:T(8,128)} fusion(s32[1024]{0:T(1024)S(1)} %bitcast.43, f32[1024,64]{1,0:T(8,128)} %bitcast.39, f32[1024]{0:T(1024)S(1)} %fusion.20, f32[]{:T(128)} %constant.76.clone.1), kind=kCustom, calls=%fused_computation.29 | custom fusion | flops 131072 | bytes 397316 | tf_op jit(solution)/shard_map/scatter-add | solution.py:90
  77.6 1.6 convert_element_type.39
  84.0 152.8 %while.13 = (s32[]{:T(128)}, f32[64,288]{1,0:T(8,128)}, s32[256,2]{0,1:T(2,128)S(1)}, f32[64,288]{1,0:T(8,128)S(1)}, f32[68,288]{1,0:T(8,128)S(1)}, /*index=5*/f...) while((s32[]{:T(128)}, f32[64,288]{1,0:T(8,128)}, ...), condition=%wide.region_6.0_spmd, body=%wide.region_0.0_spmd.sunk | while | flops 9752870 | bytes 10787303 | solution.py:74
  88.8 1.5 sub.114
  90.3 2.9 %fusion.30 = (f32[32,96,96]{2,1,0:T(8,128)S(1)}, f32[32,96,96]{2,1,0:T(8,128)S(1)}) fusion(f32[32,3,96]{2,1,0:T(4,128)} %mul.270, f32[32,3,96]{2,1,0:T(4,128)S(1)} %sub.113, f32[32,3,96]{2,1,0:T(4,128)} %sub.114), kind=kLoop, calls=%fused_computation.10.clone.1 | loop fusion | flops 3833856 | bytes 2469888 | tf_op jit(solution)/shard_map/while/body/eval_jaxpr/reduce_sum | solution.py:32
  94.0 1.7 multiply_reduce_fusion.2
  95.8 3.3 %fusion.31 = f32[32,3,96]{2,1,0:T(4,128)S(1)} fusion(f32[32,96,96]{2,1,0:T(8,128)S(1)} %get-tuple-element.217, f32[32,3,96]{2,1,0:T(4,128)S(1)} %sub.113, f32[32,3,96]{2,1,0:T(4,128)S(1)} %copy-done.2), kind=kLoop, calls=%fused_computation.11.clone.1 | loop fusion | flops 2644992 | bytes 1290240 | tf_op jit(solution)/shard_map/while/body/eval_jaxpr/reduce_sum | solution.py:34
  100.5 2.6 %scatter_custom_fusion.7 = f32[64,288]{1,0:T(8,128)} fusion(f32[64,288]{1,0:T(8,128)} %get-tuple-element.230, s32[32]{0:T(128)S(1)} %get-tuple-element.210, f32[32,288]{1,0:T(8,128)} %sub.115, f32[32]{0:T(128)S(1)} %compare_convert_fusion.2), kind=kCustom, calls=%fused_computation.16.clone.1 | custom fusion | flops 18432 | bytes 123392 | tf_op jit(solution)/shard_map/while/body/eval_jaxpr/scatter-add | solution.py:72
  107.9 1.5 sub.114
  109.4 2.9 %fusion.30 = (f32[32,96,96]{2,1,0:T(8,128)S(1)}, f32[32,96,96]{2,1,0:T(8,128)S(1)}) fusion(f32[32,3,96]{2,1,0:T(4,128)} %mul.270, f32[32,3,96]{2,1,0:T(4,128)S(1)} %sub.113, f32[32,3,96]{2,1,0:T(4,128)} %sub.114), kind=kLoop, calls=%fused_computation.10.clone.1 | loop fusion | flops 3833856 | bytes 2469888 | tf_op jit(solution)/shard_map/while/body/eval_jaxpr/reduce_sum | solution.py:32
  113.1 1.7 multiply_reduce_fusion.2
  114.9 3.3 %fusion.31 = f32[32,3,96]{2,1,0:T(4,128)S(1)} fusion(f32[32,96,96]{2,1,0:T(8,128)S(1)} %get-tuple-element.217, f32[32,3,96]{2,1,0:T(4,128)S(1)} %sub.113, f32[32,3,96]{2,1,0:T(4,128)S(1)} %copy-done.2), kind=kLoop, calls=%fused_computation.11.clone.1 | loop fusion | flops 2644992 | bytes 1290240 | tf_op jit(solution)/shard_map/while/body/eval_jaxpr/reduce_sum | solution.py:34
  119.6 2.6 %scatter_custom_fusion.7 = f32[64,288]{1,0:T(8,128)} fusion(f32[64,288]{1,0:T(8,128)} %get-tuple-element.230, s32[32]{0:T(128)S(1)} %get-tuple-element.210, f32[32,288]{1,0:T(8,128)} %sub.115, f32[32]{0:T(128)S(1)} %compare_convert_fusion.2), kind=kCustom, calls=%fused_computation.16.clone.1 | custom fusion | flops 18432 | bytes 123392 | tf_op jit(solution)/shard_map/while/body/eval_jaxpr/scatter-add | solution.py:72
  127.0 1.5 sub.114
  128.5 2.9 %fusion.30 = (f32[32,96,96]{2,1,0:T(8,128)S(1)}, f32[32,96,96]{2,1,0:T(8,128)S(1)}) fusion(f32[32,3,96]{2,1,0:T(4,128)} %mul.270, f32[32,3,96]{2,1,0:T(4,128)S(1)} %sub.113, f32[32,3,96]{2,1,0:T(4,128)} %sub.114), kind=kLoop, calls=%fused_computation.10.clone.1 | loop fusion | flops 3833856 | bytes 2469888 | tf_op jit(solution)/shard_map/while/body/eval_jaxpr/reduce_sum | solution.py:32
  132.2 1.7 multiply_reduce_fusion.2
  134.0 3.3 %fusion.31 = f32[32,3,96]{2,1,0:T(4,128)S(1)} fusion(f32[32,96,96]{2,1,0:T(8,128)S(1)} %get-tuple-element.217, f32[32,3,96]{2,1,0:T(4,128)S(1)} %sub.113, f32[32,3,96]{2,1,0:T(4,128)S(1)} %copy-done.2), kind=kLoop, calls=%fused_computation.11.clone.1 | loop fusion | flops 2644992 | bytes 1290240 | tf_op jit(solution)/shard_map/while/body/eval_jaxpr/reduce_sum | solution.py:34
  138.7 2.6 %scatter_custom_fusion.7 = f32[64,288]{1,0:T(8,128)} fusion(f32[64,288]{1,0:T(8,128)} %get-tuple-element.230, s32[32]{0:T(128)S(1)} %get-tuple-element.210, f32[32,288]{1,0:T(8,128)} %sub.115, f32[32]{0:T(128)S(1)} %compare_convert_fusion.2), kind=kCustom, calls=%fused_computation.16.clone.1 | custom fusion | flops 18432 | bytes 123392 | tf_op jit(solution)/shard_map/while/body/eval_jaxpr/scatter-add | solution.py:72
  146.1 1.5 sub.114
  147.6 2.9 %fusion.30 = (f32[32,96,96]{2,1,0:T(8,128)S(1)}, f32[32,96,96]{2,1,0:T(8,128)S(1)}) fusion(f32[32,3,96]{2,1,0:T(4,128)} %mul.270, f32[32,3,96]{2,1,0:T(4,128)S(1)} %sub.113, f32[32,3,96]{2,1,0:T(4,128)} %sub.114), kind=kLoop, calls=%fused_computation.10.clone.1 | loop fusion | flops 3833856 | bytes 2469888 | tf_op jit(solution)/shard_map/while/body/eval_jaxpr/reduce_sum | solution.py:32
  151.3 1.7 multiply_reduce_fusion.2
  153.1 3.3 %fusion.31 = f32[32,3,96]{2,1,0:T(4,128)S(1)} fusion(f32[32,96,96]{2,1,0:T(8,128)S(1)} %get-tuple-element.217, f32[32,3,96]{2,1,0:T(4,128)S(1)} %sub.113, f32[32,3,96]{2,1,0:T(4,128)S(1)} %copy-done.2), kind=kLoop, calls=%fused_computation.11.clone.1 | loop fusion | flops 2644992 | bytes 1290240 | tf_op jit(solution)/shard_map/while/body/eval_jaxpr/reduce_sum | solution.py:34
  157.8 2.6 %scatter_custom_fusion.7 = f32[64,288]{1,0:T(8,128)} fusion(f32[64,288]{1,0:T(8,128)} %get-tuple-element.230, s32[32]{0:T(128)S(1)} %get-tuple-element.210, f32[32,288]{1,0:T(8,128)} %sub.115, f32[32]{0:T(128)S(1)} %compare_convert_fusion.2), kind=kCustom, calls=%fused_computation.16.clone.1 | custom fusion | flops 18432 | bytes 123392 | tf_op jit(solution)/shard_map/while/body/eval_jaxpr/scatter-add | solution.py:72
  165.2 1.5 sub.114
  166.7 2.9 %fusion.30 = (f32[32,96,96]{2,1,0:T(8,128)S(1)}, f32[32,96,96]{2,1,0:T(8,128)S(1)}) fusion(f32[32,3,96]{2,1,0:T(4,128)} %mul.270, f32[32,3,96]{2,1,0:T(4,128)S(1)} %sub.113, f32[32,3,96]{2,1,0:T(4,128)} %sub.114), kind=kLoop, calls=%fused_computation.10.clone.1 | loop fusion | flops 3833856 | bytes 2469888 | tf_op jit(solution)/shard_map/while/body/eval_jaxpr/reduce_sum | solution.py:32
  170.4 1.7 multiply_reduce_fusion.2
  172.2 3.3 %fusion.31 = f32[32,3,96]{2,1,0:T(4,128)S(1)} fusion(f32[32,96,96]{2,1,0:T(8,128)S(1)} %get-tuple-element.217, f32[32,3,96]{2,1,0:T(4,128)S(1)} %sub.113, f32[32,3,96]{2,1,0:T(4,128)S(1)} %copy-done.2), kind=kLoop, calls=%fused_computation.11.clone.1 | loop fusion | flops 2644992 | bytes 1290240 | tf_op jit(solution)/shard_map/while/body/eval_jaxpr/reduce_sum | solution.py:34
  176.9 2.6 %scatter_custom_fusion.7 = f32[64,288]{1,0:T(8,128)} fusion(f32[64,288]{1,0:T(8,128)} %get-tuple-element.230, s32[32]{0:T(128)S(1)} %get-tuple-element.210, f32[32,288]{1,0:T(8,128)} %sub.115, f32[32]{0:T(128)S(1)} %compare_convert_fusion.2), kind=kCustom, calls=%fused_computation.16.clone.1 | custom fusion | flops 18432 | bytes 123392 | tf_op jit(solution)/shard_map/while/body/eval_jaxpr/scatter-add | solution.py:72
  184.2 1.5 sub.114
  185.8 2.9 %fusion.30 = (f32[32,96,96]{2,1,0:T(8,128)S(1)}, f32[32,96,96]{2,1,0:T(8,128)S(1)}) fusion(f32[32,3,96]{2,1,0:T(4,128)} %mul.270, f32[32,3,96]{2,1,0:T(4,128)S(1)} %sub.113, f32[32,3,96]{2,1,0:T(4,128)} %sub.114), kind=kLoop, calls=%fused_computation.10.clone.1 | loop fusion | flops 3833856 | bytes 2469888 | tf_op jit(solution)/shard_map/while/body/eval_jaxpr/reduce_sum | solution.py:32
  189.5 1.7 multiply_reduce_fusion.2
  191.3 3.3 %fusion.31 = f32[32,3,96]{2,1,0:T(4,128)S(1)} fusion(f32[32,96,96]{2,1,0:T(8,128)S(1)} %get-tuple-element.217, f32[32,3,96]{2,1,0:T(4,128)S(1)} %sub.113, f32[32,3,96]{2,1,0:T(4,128)S(1)} %copy-done.2), kind=kLoop, calls=%fused_computation.11.clone.1 | loop fusion | flops 2644992 | bytes 1290240 | tf_op jit(solution)/shard_map/while/body/eval_jaxpr/reduce_sum | solution.py:34
  196.0 2.6 %scatter_custom_fusion.7 = f32[64,288]{1,0:T(8,128)} fusion(f32[64,288]{1,0:T(8,128)} %get-tuple-element.230, s32[32]{0:T(128)S(1)} %get-tuple-element.210, f32[32,288]{1,0:T(8,128)} %sub.115, f32[32]{0:T(128)S(1)} %compare_convert_fusion.2), kind=kCustom, calls=%fused_computation.16.clone.1 | custom fusion | flops 18432 | bytes 123392 | tf_op jit(solution)/shard_map/while/body/eval_jaxpr/scatter-add | solution.py:72
  204.9 2.9 %fusion.30 = (f32[32,96,96]{2,1,0:T(8,128)S(1)}, f32[32,96,96]{2,1,0:T(8,128)S(1)}) fusion(f32[32,3,96]{2,1,0:T(4,128)} %mul.270, f32[32,3,96]{2,1,0:T(4,128)S(1)} %sub.113, f32[32,3,96]{2,1,0:T(4,128)} %sub.114), kind=kLoop, calls=%fused_computation.10.clone.1 | loop fusion | flops 3833856 | bytes 2469888 | tf_op jit(solution)/shard_map/while/body/eval_jaxpr/reduce_sum | solution.py:32
  208.6 1.7 multiply_reduce_fusion.2
  210.4 3.3 %fusion.31 = f32[32,3,96]{2,1,0:T(4,128)S(1)} fusion(f32[32,96,96]{2,1,0:T(8,128)S(1)} %get-tuple-element.217, f32[32,3,96]{2,1,0:T(4,128)S(1)} %sub.113, f32[32,3,96]{2,1,0:T(4,128)S(1)} %copy-done.2), kind=kLoop, calls=%fused_computation.11.clone.1 | loop fusion | flops 2644992 | bytes 1290240 | tf_op jit(solution)/shard_map/while/body/eval_jaxpr/reduce_sum | solution.py:34
  215.1 2.6 %scatter_custom_fusion.7 = f32[64,288]{1,0:T(8,128)} fusion(f32[64,288]{1,0:T(8,128)} %get-tuple-element.230, s32[32]{0:T(128)S(1)} %get-tuple-element.210, f32[32,288]{1,0:T(8,128)} %sub.115, f32[32]{0:T(128)S(1)} %compare_convert_fusion.2), kind=kCustom, calls=%fused_computation.16.clone.1 | custom fusion | flops 18432 | bytes 123392 | tf_op jit(solution)/shard_map/while/body/eval_jaxpr/scatter-add | solution.py:72
  222.4 1.5 sub.114
  224.0 2.9 %fusion.30 = (f32[32,96,96]{2,1,0:T(8,128)S(1)}, f32[32,96,96]{2,1,0:T(8,128)S(1)}) fusion(f32[32,3,96]{2,1,0:T(4,128)} %mul.270, f32[32,3,96]{2,1,0:T(4,128)S(1)} %sub.113, f32[32,3,96]{2,1,0:T(4,128)} %sub.114), kind=kLoop, calls=%fused_computation.10.clone.1 | loop fusion | flops 3833856 | bytes 2469888 | tf_op jit(solution)/shard_map/while/body/eval_jaxpr/reduce_sum | solution.py:32
  227.7 1.7 multiply_reduce_fusion.2
  229.5 3.3 %fusion.31 = f32[32,3,96]{2,1,0:T(4,128)S(1)} fusion(f32[32,96,96]{2,1,0:T(8,128)S(1)} %get-tuple-element.217, f32[32,3,96]{2,1,0:T(4,128)S(1)} %sub.113, f32[32,3,96]{2,1,0:T(4,128)S(1)} %copy-done.2), kind=kLoop, calls=%fused_computation.11.clone.1 | loop fusion | flops 2644992 | bytes 1290240 | tf_op jit(solution)/shard_map/while/body/eval_jaxpr/reduce_sum | solution.py:34
  234.2 2.6 %scatter_custom_fusion.7 = f32[64,288]{1,0:T(8,128)} fusion(f32[64,288]{1,0:T(8,128)} %get-tuple-element.230, s32[32]{0:T(128)S(1)} %get-tuple-element.210, f32[32,288]{1,0:T(8,128)} %sub.115, f32[32]{0:T(128)S(1)} %compare_convert_fusion.2), kind=kCustom, calls=%fused_computation.16.clone.1 | custom fusion | flops 18432 | bytes 123392 | tf_op jit(solution)/shard_map/while/body/eval_jaxpr/scatter-add | solution.py:72
  (166 shorter events, 68.6 us)
Async XLA Ops:
  7.2 40.5 %copy-start = (bf16[64,288,64]{1,2,0:T(8,128)(2,1)S(1)}, bf16[64,288,64]{1,2,0:T(8,128)(2,1)}, u32[]{:S(2)}) copy-start(bf16[64,288,64]{1,2,0:T(8,128)(2,1)} %param.14) | copy-start | bytes 7077892
  7.2 229.6 %all-reduce.2.cloned.1.call-start = ((), (), s32[]{:S(2)}) async-start(), calls=%async_computation | async-start | bytes 262144 | tf_op jit(solution)/shard_map/psum | solution.py:92
  8.7 73.9 %collective-permute-start.1 = (f32[2,2,288]{2,1,0:T(2,128)}, f32[2,2,288]{2,1,0:T(2,128)}, u32[]{:S(2)}, u32[]{:S(2)}) collective-permute-start(f32[2,2,288]{2,1,0:T(2,128)} %get-tuple-element.156), channel_id=1, source_target_pairs={{1,0},{2,1},{3,2},{4,3},{5,4},{6,5},{7,6},{8,7},{9,8},{10,9},{11,1... | collective-permute-start | bytes 13832 | tf_op jit(solution)/shard_map/ppermute | solution.py:22
  10.0 72.6 %collective-permute-start = (f32[2,2,288]{2,1,0:T(2,128)S(1)}, f32[2,2,288]{2,1,0:T(2,128)}, u32[]{:S(2)}, u32[]{:S(2)}) collective-permute-start(f32[2,2,288]{2,1,0:T(2,128)S(1)} %get-tuple-element.155), channel_id=1, source_target_pairs={{0,1},{1,2},{2,3},{3,4},{4,5},{5,6},{6,7},{7,8},{8,9},{9,10},{10,1... | collective-permute-start | bytes 13832 | tf_op jit(solution)/shard_map/ppermute | solution.py:21
  61.1 21.5 %copy-start.1 = (f32[64,288]{1,0:T(8,128)S(1)}, f32[64,288]{1,0:T(8,128)}, u32[]{:S(2)}) copy-start(f32[64,288]{1,0:T(8,128)} %param.13) | copy-start | bytes 221188
  61.1 21.5 %copy-start.4 = (f32[64,288]{1,0:T(8,128)S(1)}, f32[64,288]{1,0:T(8,128)}, u32[]{:S(2)}) copy-start(f32[64,288]{1,0:T(8,128)} %param.12) | copy-start | bytes 221188
  70.0 14.0 %copy-start.8 = (s32[256,2]{0,1:T(2,128)S(1)}, s32[256,2]{0,1:T(2,128)}, u32[]{:S(2)}) copy-start(s32[256,2]{0,1:T(2,128)} %param.15) | copy-start | bytes 6148
  93.2 0.8 copy-start.3
  93.2 2.6 %copy-start.2 = (f32[32,3,96]{2,1,0:T(4,128)S(1)}, f32[32,3,96]{2,1,0:T(4,128)}, u32[]{:S(2)}) copy-start(f32[32,3,96]{2,1,0:T(4,128)} %sub.114) | copy-start | bytes 110596 | tf_op jit(solution)/shard_map/while
  112.3 0.8 copy-start.3
  112.3 2.6 %copy-start.2 = (f32[32,3,96]{2,1,0:T(4,128)S(1)}, f32[32,3,96]{2,1,0:T(4,128)}, u32[]{:S(2)}) copy-start(f32[32,3,96]{2,1,0:T(4,128)} %sub.114) | copy-start | bytes 110596 | tf_op jit(solution)/shard_map/while
  131.4 0.8 copy-start.3
  131.4 2.6 %copy-start.2 = (f32[32,3,96]{2,1,0:T(4,128)S(1)}, f32[32,3,96]{2,1,0:T(4,128)}, u32[]{:S(2)}) copy-start(f32[32,3,96]{2,1,0:T(4,128)} %sub.114) | copy-start | bytes 110596 | tf_op jit(solution)/shard_map/while
  150.5 0.8 copy-start.3
  150.5 2.6 %copy-start.2 = (f32[32,3,96]{2,1,0:T(4,128)S(1)}, f32[32,3,96]{2,1,0:T(4,128)}, u32[]{:S(2)}) copy-start(f32[32,3,96]{2,1,0:T(4,128)} %sub.114) | copy-start | bytes 110596 | tf_op jit(solution)/shard_map/while
  169.6 0.8 copy-start.3
  169.6 2.6 %copy-start.2 = (f32[32,3,96]{2,1,0:T(4,128)S(1)}, f32[32,3,96]{2,1,0:T(4,128)}, u32[]{:S(2)}) copy-start(f32[32,3,96]{2,1,0:T(4,128)} %sub.114) | copy-start | bytes 110596 | tf_op jit(solution)/shard_map/while
  188.7 0.8 copy-start.3
  188.7 2.6 %copy-start.2 = (f32[32,3,96]{2,1,0:T(4,128)S(1)}, f32[32,3,96]{2,1,0:T(4,128)}, u32[]{:S(2)}) copy-start(f32[32,3,96]{2,1,0:T(4,128)} %sub.114) | copy-start | bytes 110596 | tf_op jit(solution)/shard_map/while
  207.8 0.8 copy-start.3
  207.8 2.6 %copy-start.2 = (f32[32,3,96]{2,1,0:T(4,128)S(1)}, f32[32,3,96]{2,1,0:T(4,128)}, u32[]{:S(2)}) copy-start(f32[32,3,96]{2,1,0:T(4,128)} %sub.114) | copy-start | bytes 110596 | tf_op jit(solution)/shard_map/while
  226.9 0.8 copy-start.3
  226.9 2.6 %copy-start.2 = (f32[32,3,96]{2,1,0:T(4,128)S(1)}, f32[32,3,96]{2,1,0:T(4,128)}, u32[]{:S(2)}) copy-start(f32[32,3,96]{2,1,0:T(4,128)} %sub.114) | copy-start | bytes 110596 | tf_op jit(solution)/shard_map/while
  236.8 1.5 copy-start.5
  236.8 1.5 copy-start.6
  236.8 1.5 copy-start.7
Sparse Core Ops, SparseCore 0:
  79.4 71.2 all-reduce.1
where the time goes:
time: 249 us; the launch traced here: 246 us
  other arithmetic  111 us (45%)
  local copies, waits for them, and re-layouts  94.3 us (38%)
  between operations  14.8 us (6%)
  matrix products  10.7 us (4%)
  starting transfers between devices  7.38 us (3%)
  blocking collectives  7.29 us (3%)
    unnamed x15, local copies, waits for them, and re-layouts  29.2 us
    reduce_sum x8, other arithmetic, kernel_block(): jnp.sum(offsets * (along * inverse / distance)[:, None, :, :], axis=3)  26.6 us
    reduce_sum x8, other arithmetic, kernel_block(): along = jnp.sum(offsets * source_disp[:, :, None, :], axis=1)  23.3 us
    scatter-add x8, other arithmetic, near_step(): return summed.at[targets].add(contrib.reshape(group_size, row_width))  20.8 us
    sub x16, local copies, waits for them, and re-layouts, kernel_block(): offsets = target_pos[:, :, :, None] - source_pos[:, :, None, :]  19.2 us
    reduce_sum x8, other arithmetic, kernel_block(): jnp.sum(inverse[:, None, :, :] * source_disp[:, :, None, :], axis=3)  13.9 us
    gather x8, local copies, waits for them, and re-layouts, near_step(): target_pos = positions[targets].reshape(group_size, 3, elems)  9.73 us
    gather x8, local copies, waits for them, and re-layouts, near_step(): source_pos = ext_pos[sources].reshape(group_size, 3, elems)  9.65 us
  transfers between devices with their start and end apart: 3, of which 0 were waited for; matrix products, arithmetic and copies ran while one was open for 85% of the time, Pallas kernels for 0%

commit v1 on v0

v1 whole, which is shorter than its diff:
```python
import functools

import jax
import jax.numpy as jnp
from jax import lax
from jax.experimental import pallas as pl
from jax.experimental.pallas import tpu as pltpu
from jax.sharding import PartitionSpec as P

HALO = 2
LANES = 128
SUBLANES = 8
CHUNK = 32
GROUPS = LANES // CHUNK
core_square = 0.25
softening = 1.5
UNROLL = 2
VMEM = 56 * 1024 * 1024


def near_kernel(
    pairs_ref,
    count_ref,
    disp_ref,
    pos_ref,
    before_ref,
    after_ref,
    intact_ref,
    stiff_ref,
    out_ref,
    damage_ref,
    ext_scr,
    src_scr,
    tgt_scr,
    acc_scr,
):
    clusters, width = disp_ref.shape
    elems = width // 3
    chunks = elems // CHUNK
    steps = elems // (GROUPS * SUBLANES)
    spread = elems // GROUPS
    halo = before_ref.shape[0] // 2
    sources = clusters + 2 * halo
    tiles = ext_scr.shape[2] // LANES
    lane = lax.broadcasted_iota(jnp.int32, (SUBLANES, LANES), 1)
    group = lane // CHUNK
    group_start = group * CHUNK

    for k, own in enumerate((disp_ref, pos_ref)):
        ext_scr[k, 0:halo, 0:width] = before_ref[k * halo : (k + 1) * halo, :]
        ext_scr[k, halo : halo + clusters, 0:width] = own[...]
        ext_scr[k, halo + clusters : sources, 0:width] = after_ref[k * halo : (k + 1) * halo, :]

    flipped = [
        jnp.concatenate(
            [ext_scr[k, :, t * LANES : (t + 1) * LANES].T for t in range(tiles)], axis=0
        )
        for k in range(2)
    ]
    for block in range(pl.cdiv(sources, CHUNK)):
        packed = []
        for k in (1, 0):
            for c in range(3):
                for f in range(steps):
                    merged = None
                    for g in range(GROUPS):
                        row = c * elems + g * spread + f * SUBLANES
                        piece = flipped[k][row : row + SUBLANES, :]
                        shift = (g * CHUNK - block * CHUNK) % LANES
                        if shift:
                            piece = pltpu.roll(piece, shift, 1)
                        merged = piece if merged is None else jnp.where(group == g, piece, merged)
                    packed.append(merged)
        for i in range(min(CHUNK, sources - block * CHUNK)):
            index = group_start + i
            for n, item in enumerate(packed):
                value = jnp.take_along_axis(item, index, axis=1, mode="promise_in_bounds")
                src_scr[block * CHUNK + i, n] = value
                if n >= 3 * steps:
                    src_scr[block * CHUNK + i, n + 3 * steps] = 3.0 * value

    within = lax.broadcasted_iota(jnp.int32, (clusters, LANES), 1) % CHUNK
    for m in range(3 * chunks):
        tile = m // GROUPS
        own = ext_scr[1, halo : halo + clusters, tile * LANES : (tile + 1) * LANES]
        tgt_scr[:, m, :] = jnp.take_along_axis(
            own, within + (m % GROUPS) * CHUNK, axis=1, mode="promise_in_bounds"
        )

    acc_scr[...] = jnp.zeros_like(acc_scr)
    count = count_ref[0]

    def one_pair(slot):
        target = pairs_ref[0, slot]
        source = pairs_ref[1, slot]
        into = jnp.where(slot < count, target, clusters) * SUBLANES
        into = pl.multiple_of(into, SUBLANES)
        tgt = [
            jnp.broadcast_to(tgt_scr[target, m : m + 1, :], (SUBLANES, LANES))
            for m in range(3 * chunks)
        ]
        sums = [None] * (3 * chunks)
        for f in range(steps):
            y = [src_scr[source, c * steps + f] for c in range(3)]
            u = [src_scr[source, (3 + c) * steps + f] for c in range(3)]
            v = [src_scr[source, (6 + c) * steps + f] for c in range(3)]
            for h in range(chunks):
                r = [tgt[c * chunks + h] - y[c] for c in range(3)]
                q = (r[0] * r[0] + core_square) + (r[1] * r[1] + r[2] * r[2])
                s = r[0] * v[0] + (r[1] * v[1] + r[2] * v[2])
                inverse = lax.rsqrt(q)
                square = inverse * inverse
                weight = square * inverse
                s = s * square
                for c in range(3):
                    term = weight * (u[c] - s * r[c])
                    m = c * chunks + h
                    sums[m] = term if sums[m] is None else sums[m] + term
        for m in range(3 * chunks):
            acc_scr[m, pl.ds(into, SUBLANES), :] += sums[m]

    def step(it, carry):
        for k in range(UNROLL):
            one_pair(it * UNROLL + k)
        return carry

    lax.fori_loop(0, (count + UNROLL - 1) // UNROLL, step, 0)

    own_group = lax.broadcasted_iota(jnp.int32, (clusters, LANES), 1) // CHUNK
    for t in range(tiles):
        merged = None
        for g in range(GROUPS):
            m = t * GROUPS + g
            if m >= 3 * chunks:
                break
            total = acc_scr[m, pl.ds(0, clusters, stride=SUBLANES), :]
            for s in range(1, SUBLANES):
                total = total + acc_scr[m, pl.ds(s, clusters, stride=SUBLANES), :]
            total = total + pltpu.roll(total, 2 * CHUNK, 1)
            total = total + pltpu.roll(total, CHUNK, 1)
            merged = total if merged is None else jnp.where(own_group == g, total, merged)
        ext_scr[0, 0:clusters, t * LANES : (t + 1) * LANES] = merged

    disp = [disp_ref[:, c * elems : (c + 1) * elems] for c in range(3)]
    separation = jnp.sqrt(1.0 + (disp[0] * disp[0] + disp[1] * disp[1] + disp[2] * disp[2]))
    softened = 1.0 - jnp.exp(-(separation - 1.0) / softening)
    intact = intact_ref[...].astype(jnp.float32)
    damage = intact * softened + (1.0 - intact)
    damage_ref[...] = damage
    hold = (1.0 - damage) * stiff_ref[...]
    for c in range(3):
        near = ext_scr[0, 0:clusters, c * elems : (c + 1) * elems]
        out_ref[:, c * elems : (c + 1) * elems] = near - hold * disp[c]


def near_field(pairs, count, disp, pos, before, after, intact, stiffness):
    clusters, width = disp.shape
    elems = width // 3
    chunks = elems // CHUNK
    steps = elems // (GROUPS * SUBLANES)
    halo = before.shape[0] // 2
    sources = clusters + 2 * halo
    padded = pl.cdiv(width, LANES) * LANES
    slots = pairs.shape[1]
    vmem = pl.BlockSpec(memory_space=pltpu.VMEM)
    smem = pl.BlockSpec(memory_space=pltpu.SMEM)
    return pl.pallas_call(
        near_kernel,
        out_shape=(
            jax.ShapeDtypeStruct((clusters, width), jnp.float32),
            jax.ShapeDtypeStruct((clusters, elems), jnp.float32),
        ),
        in_specs=[smem, smem] + [vmem] * 6,
        out_specs=(vmem, vmem),
        scratch_shapes=[
            pltpu.VMEM((2, LANES, padded), jnp.float32),
            pltpu.VMEM((sources, 9 * steps, SUBLANES, LANES), jnp.float32),
            pltpu.VMEM((clusters, 3 * chunks, LANES), jnp.float32),
            pltpu.VMEM((3 * chunks, (clusters + 1) * SUBLANES, LANES), jnp.float32),
        ],
        compiler_params=pltpu.CompilerParams(vmem_limit_bytes=VMEM),
        cost_estimate=pl.CostEstimate(
            flops=30 * slots * elems * elems,
            bytes_accessed=4 * clusters * width * 6,
            transcendentals=slots * elems * elems,
        ),
        name="near_field",
    )(pairs, count, disp, pos, before, after, intact, stiffness)


def far_kernel(
    count_ref, column_ref, pairs_ref, blocks_ref, out_ref, coeff_scr, sum_scr, *, steps
):
    step = pl.program_id(0)
    rows, rank, slots = blocks_ref.shape
    sources = column_ref.shape[0]
    targets = out_ref.shape[0]

    @pl.when(step == 0)
    def _():
        chosen = pairs_ref[1:2, :]
        index = lax.broadcasted_iota(jnp.int32, (sources, slots), 0)
        pick = jnp.where(index == chosen, 1.0, 0.0).astype(jnp.bfloat16)
        coeff_scr[...] = lax.dot_general(
            column_ref[...], pick, (((0,), (0,)), ((), ())), preferred_element_type=jnp.float32
        )

    for t in range(slots // LANES):
        lanes = slice(t * LANES, (t + 1) * LANES)
        coeff = coeff_scr[:, lanes]
        for r in range(rows):
            product = blocks_ref[r, :, lanes].astype(jnp.float32) * coeff
            folded = product[0:SUBLANES]
            for s in range(1, rank // SUBLANES):
                folded = folded + product[s * SUBLANES : (s + 1) * SUBLANES]
            start = pl.multiple_of((step * rows + r) * SUBLANES, SUBLANES)
            sum_scr[t, pl.ds(start, SUBLANES), :] = folded

    @pl.when(step == steps - 1)
    def _():
        parts = []
        for t in range(slots // LANES):
            total = sum_scr[t, pl.ds(0, rank, stride=SUBLANES), :]
            for s in range(1, SUBLANES):
                total = total + sum_scr[t, pl.ds(s, rank, stride=SUBLANES), :]
            parts.append(total)
        coupled = jnp.concatenate(parts, axis=1)
        high = coupled.astype(jnp.bfloat16)
        low = (coupled - high.astype(jnp.float32)).astype(jnp.bfloat16)
        both = jnp.concatenate([high, low], axis=0)
        slot = lax.broadcasted_iota(jnp.int32, (1, slots), 1)
        wanted = jnp.where(slot < count_ref[0], pairs_ref[0:1, :], -1)
        index = lax.broadcasted_iota(jnp.int32, (targets, slots), 0)
        place = jnp.where(index == wanted, 1.0, 0.0).astype(jnp.bfloat16)
        summed = lax.dot_general(
            place, both, (((1,), (1,)), ((), ())), preferred_element_type=jnp.float32
        )
        out_ref[...] = (summed[:, 0:rank] + summed[:, rank:]).astype(out_ref.dtype)


def far_field(count, column, pairs, blocks, targets):
    rank, _, slots = blocks.shape
    sources = column.shape[0]
    rows = SUBLANES
    steps = rank // rows
    vmem = pl.BlockSpec(memory_space=pltpu.VMEM)
    smem = pl.BlockSpec(memory_space=pltpu.SMEM)
    return pl.pallas_call(
        functools.partial(far_kernel, steps=steps),
        grid=(steps,),
        out_shape=jax.ShapeDtypeStruct((targets, rank), jnp.bfloat16),
        in_specs=[
            smem,
            vmem,
            vmem,
            pl.BlockSpec((rows, rank, slots), lambda i: (i, 0, 0)),
        ],
        out_specs=pl.BlockSpec((targets, rank), lambda i: (0, 0)),
        scratch_shapes=[
            pltpu.VMEM((rank, slots), jnp.float32),
            pltpu.VMEM((slots // LANES, rank * SUBLANES, LANES), jnp.float32),
        ],
        compiler_params=pltpu.CompilerParams(vmem_limit_bytes=VMEM),
        cost_estimate=pl.CostEstimate(
            flops=2 * rank * rank * slots,
            bytes_accessed=2 * rank * rank * slots,
            transcendentals=0,
        ),
        name="far_field",
    )(count, column, pairs, blocks)


def local(
    displacement,
    positions,
    cluster_basis,
    near_pairs,
    near_count,
    far_pairs,
    far_count,
    far_blocks,
    intact,
    stiffness,
):
    clusters = displacement.shape[0]
    rank = cluster_basis.shape[2]
    cols = lax.axis_size("cols")
    devices = lax.axis_size("rows") * cols
    axes = ("rows", "cols")

    up = [(i, i + 1) for i in range(devices - 1)]
    down = [(i + 1, i) for i in range(devices - 1)]
    last = jnp.concatenate([displacement[clusters - HALO :], positions[clusters - HALO :]], axis=0)
    first = jnp.concatenate([displacement[:HALO], positions[:HALO]], axis=0)
    before = lax.ppermute(last, axes, up)
    after = lax.ppermute(first, axes, down)

    disp_bf = displacement.astype(jnp.bfloat16)
    coeff = jnp.einsum("kf,kfr->kr", disp_bf, cluster_basis, preferred_element_type=jnp.float32)
    column = lax.all_gather(coeff.astype(jnp.bfloat16), "rows", axis=0, tiled=True)
    partial = far_field(
        far_count, column, far_pairs.T, far_blocks.transpose(1, 2, 0), clusters * cols
    )
    received = lax.all_to_all(
        partial.reshape(cols, clusters, rank), "cols", split_axis=0, concat_axis=0
    )

    near, damage = near_field(
        near_pairs.T, near_count, displacement, positions, before, after, intact, stiffness
    )
    owned = jnp.sum(received.astype(jnp.float32), axis=0).astype(jnp.bfloat16)
    far_part = jnp.einsum("kfr,kr->kf", cluster_basis, owned, preferred_element_type=jnp.float32)
    return (near + far_part, damage)


def solution(mesh):
    both = ("rows", "cols")
    in_specs = (
        P(both, None),
        P(both, None),
        P(both, None, None),
        P(both, None),
        P(both),
        P(both, None),
        P(both),
        P(both, None, None),
        P(both, None),
        P(both, None),
    )
    out_specs = (P(both, None), P(both, None))
    return jax.shard_map(local, mesh=mesh, in_specs=in_specs, out_specs=out_specs, check_vma=False)
```

time: 249 us -> 53.8 us (0.22)
  the two profiles are of different devices: /device:TPU:0 before, /device:TPU:22 now
where the time goes in v1:
time: 53.8 us; the launch traced here: 53.2 us
  Pallas kernels  24.2 us (45%)
  starting transfers between devices  11.2 us (21%)
  blocking collectives  5.7 us (11%)
  local copies, waits for them, and re-layouts  3.4 us (6%)
  waiting for transfers between devices  3.28 us (6%)
  between operations  2 us (4%)
  matrix products  1.82 us (3%)
  other arithmetic  1.61 us (3%)
    pallas_call x1, Pallas kernels, near_field(): pl.pallas_call(near_kernel, out_shape=(jax.ShapeDtypeStruct((clusters, wi...  16.2 us
    pallas_call x1, Pallas kernels, far_field(): pl.pallas_call(functools.partial(far_kernel, steps=steps), grid=(steps,),...  8.04 us
    all_gather x1, blocking collectives, local(): lax.all_gather(coeff.astype(jnp.bfloat16), 'rows', axis=0, tiled=True)  5.7 us
    all_to_all x1, starting transfers between devices, local(): lax.all_to_all(partial.reshape(cols, clusters, rank), 'cols', split_axis=...  5.13 us
    ppermute x1, starting transfers between devices, local(): before = lax.ppermute(last, axes, up)  3.59 us
    ppermute x1, waiting for transfers between devices, local(): after = lax.ppermute(first, axes, down)  3.28 us
    unnamed x10, local copies, waits for them, and re-layouts  2.48 us
    ppermute x1, starting transfers between devices, local(): after = lax.ppermute(first, axes, down)  2.47 us
  transfers between devices with their start and end apart: 3, of which 1 were waited for; matrix products, arithmetic and copies ran while one was open for 7% of the time, Pallas kernels for 45%

profile of v1, /device:TPU:22, one launch (start us, length us, event | category | flops | bytes accessed | tf_op | source)
XLA Modules:
  0.0 53.2 jit_solution(9650589912919485921)
XLA Ops:
  0.6 0.0 copy-start
  0.6 0.9 %fusion.4 = (f32[2,288]{1,0:T(2,128)S(1)}, f32[2,288]{1,0:T(2,128)S(1)}, f32[2,288]{1,0:T(2,128)S(1)}, f32[2,288]{1,0:T(2,128)S(1)}) fusion(f32[64,288]{1,0:T(8,128)} %disp_ref.1, f32[64,288]{1,0:T(8,128)} %pos_ref.1), kind=kLoop, calls=%fused_computation.8 | loop fusion | bytes 18432 | tf_op jit(solution)/shard_map/slice | solution.py:294
  1.6 3.6 %collective-permute-start = (f32[4,288]{1,0:T(4,128)S(1)}, f32[4,288]{1,0:T(4,128)S(1)}, u32[]{:S(2)}, u32[]{:S(2)}) collective-permute-start(f32[4,288]{1,0:T(4,128)S(1)} %pad_maximum_fusion), channel_id=1, source_target_pairs={{0,1},{1,2},{2,3},{3,4},{4,5},{5,6},{6,7},{7,8},{8,9},{9,10},{10,1... | collective-permute-start | bytes 13832 | tf_op jit(solution)/shard_map/ppermute | solution.py:295
  5.2 0.9 %convert_bitcast_fusion = bf16[64,288,1]{1,0,2:T(8,128)(2,1)S(1)} fusion(f32[64,288]{1,0:T(8,128)} %disp_ref.1), kind=kLoop, calls=%fused_computation.3 | loop fusion | flops 18432 | bytes 110592 | tf_op jit(solution)/shard_map/convert_element_type | solution.py:298
  6.7 0.0 copy-done
  6.7 1.2 %fusion = f32[64,1,64]{2,1,0:T(1,128)S(1)} fusion(bf16[64,288,64]{1,2,0:T(8,128)(2,1)S(1)} %copy-done, bf16[64,288,1]{1,0,2:T(8,128)(2,1)S(1)} %convert_bitcast_fusion), kind=kOutput, calls=%fused_computation.1 | convolution fusion | flops 2359296 | bytes 2412544 | tf_op jit(solution)/shard_map/kf,kfr->kr/dot_general | solution.py:299
  7.9 5.7 %all_gather.3.column_ref = bf16[256,64]{1,0:T(8,128)(2,1)} all-gather(bf16[64,64]{1,0:T(8,128)(2,1)S(1)} %convert_element_type.9), channel_id=1, replica_groups=mesh['rows'=4,'cols'=8] {'rows'}, dimensions={0}, use_global_device_ids=true | all-gather | bytes 40960 | tf_op jit(solution)/shard_map/all_gather | solution.py:300
  13.6 8.0 %far_field.1 = bf16[512,64]{1,0:T(8,128)(2,1)} custom-call(s32[1]{0:T(128)S(6)} %copy.22.count_ref, bf16[256,64]{1,0:T(8,128)(2,1)} %all_gather.3.column_ref, s32[2,1024]{1,0:T(2,128)} %bitcast.17, bf16[64,64,1024]{2,1,0:T(8,128)(2,1)} %bitcast.13), custom_call_target="tpu_custom_call" | custom-call | flops 8388608 | bytes 8388608 | tf_op jit(solution)/shard_map/far_field/pallas_call | solution.py:248
  21.7 1.7 %reshape.12 = bf16[8,2,2048]{2,1,0:T(2,128)(2,1)} reshape(bf16[8,64,64]{2,1,0:T(8,128)(2,1)} %bitcast.14) | data formatting | bytes 131072
  23.3 5.1 %all-to-all-start = ((bf16[8,2,2048]{2,1,0:T(2,128)(2,1)}), bf16[8,2,2048]{2,1,0:T(2,128)(2,1)S(1)}, u32[]{:S(2)}, u32[]{:S(2)}) async-start(bf16[8,2,2048]{2,1,0:T(2,128)(2,1)} %reshape.12), calls=%async_computation | async-start | bytes 131072 | tf_op jit(solution)/shard_map/all_to_all | solution.py:304
  28.5 2.5 %collective-permute-start.1 = (f32[4,288]{1,0:T(4,128)S(1)}, f32[4,288]{1,0:T(4,128)S(1)}, u32[]{:S(2)}, u32[]{:S(2)}) collective-permute-start(f32[4,288]{1,0:T(4,128)S(1)} %pad_maximum_fusion.1), channel_id=1, source_target_pairs={{1,0},{2,1},{3,2},{4,3},{5,4},{6,5},{7,6},{8,7},{9,8},{10,9},{11,1... | collective-permute-start | bytes 13832 | tf_op jit(solution)/shard_map/ppermute | solution.py:296
  31.6 0.0 collective-permute-done.before_ref
  31.6 0.0 copy-start.2
  31.6 3.3 %collective-permute-done.1.after_ref = f32[4,288]{1,0:T(4,128)S(1)} collective-permute-done((f32[4,288]{1,0:T(4,128)S(1)}, f32[4,288]{1,0:T(4,128)S(1)}, u32[]{:S(2)}, u32[]{:S(2)}) %collective-permute-start.1) | collective-permute-done | bytes 4640 | tf_op jit(solution)/shard_map/ppermute | solution.py:296
  34.9 0.0 copy-start.3
  34.9 0.0 copy-done.2
  34.9 0.6 %copy-done.3 = f32[4,288]{1,0:T(4,128)} copy-done((f32[4,288]{1,0:T(4,128)}, f32[4,288]{1,0:T(4,128)S(1)}, u32[]{:S(2)}) %copy-start.3) | copy-done | bytes 4632
  35.5 16.2 %near_field.1 = (f32[64,288]{1,0:T(8,128)}, f32[64,96]{1,0:T(8,128)}) custom-call(s32[2,256]{1,0:T(2,128)} %bitcast.18, s32[1]{0:T(128)S(6)} %copy.21.count_ref, f32[64,288]{1,0:T(8,128)} %disp_ref.1, f32[64,288]{1,0:T(8,128)} %pos_ref.1, f32[4,288]{1,0:T(4,128)} %copy-done.2, f32[4,288]{1,0:T(4,128)} %copy-done.3, s32[64,96]{1,0:T(8,128)} %intact_ref.1, ...), custom_call_target="tpu_custom_call" | custom-call | flops 70778880 | bytes 442368 | tf_op jit(solution)/shard_map/near_field/pallas_call | solution.py:167
  51.7 0.0 copy-start.1
  51.7 0.0 all-to-all-done
  51.7 0.1 reshape.13
  51.9 0.6 %fusion.2 = f32[64,1,288]{2,1,0:T(1,128)S(1)} fusion(bf16[64,288,64]{1,2,0:T(8,128)(2,1)S(1)} %copy-done, bf16[64,64,1]{1,0,2:T(8,128)(2,1)S(1)} %bitcast.15), kind=kOutput, calls=%fused_computation.4 | convolution fusion | flops 2359296 | bytes 2441216 | tf_op jit(solution)/shard_map/kfr,kr->kf/dot_general | solution.py:312
  52.5 0.1 copy-done.1
  52.5 0.7 %bitcast_add_fusion = f32[64,288]{1,0:T(8,128)} fusion(f32[64,288]{1,0:T(8,128)S(1)} %copy-done.1, f32[64,1,288]{2,1,0:T(1,128)S(1)} %fusion.2), kind=kLoop, calls=%fused_computation | loop fusion | flops 18432 | bytes 221184 | tf_op jit(solution)/shard_map/add | solution.py:313
  (4 shorter events, 0.1 us)
Async XLA Ops:
  0.6 6.1 %copy-start = (bf16[64,288,64]{1,2,0:T(8,128)(2,1)S(1)}, bf16[64,288,64]{1,2,0:T(8,128)(2,1)}, u32[]{:S(2)}) copy-start(bf16[64,288,64]{1,2,0:T(8,128)(2,1)} %param.12) | copy-start | bytes 7077892
  1.6 30.0 %collective-permute-start = (f32[4,288]{1,0:T(4,128)S(1)}, f32[4,288]{1,0:T(4,128)S(1)}, u32[]{:S(2)}, u32[]{:S(2)}) collective-permute-start(f32[4,288]{1,0:T(4,128)S(1)} %pad_maximum_fusion), channel_id=1, source_target_pairs={{0,1},{1,2},{2,3},{3,4},{4,5},{5,6},{6,7},{7,8},{8,9},{9,10},{10,1... | collective-permute-start | bytes 13832 | tf_op jit(solution)/shard_map/ppermute | solution.py:295
  23.3 28.3 %all-to-all-start = ((bf16[8,2,2048]{2,1,0:T(2,128)(2,1)}), bf16[8,2,2048]{2,1,0:T(2,128)(2,1)S(1)}, u32[]{:S(2)}, u32[]{:S(2)}) async-start(bf16[8,2,2048]{2,1,0:T(2,128)(2,1)} %reshape.12), calls=%async_computation | async-start | bytes 131072 | tf_op jit(solution)/shard_map/all_to_all | solution.py:304
  28.5 6.4 %collective-permute-start.1 = (f32[4,288]{1,0:T(4,128)S(1)}, f32[4,288]{1,0:T(4,128)S(1)}, u32[]{:S(2)}, u32[]{:S(2)}) collective-permute-start(f32[4,288]{1,0:T(4,128)S(1)} %pad_maximum_fusion.1), channel_id=1, source_target_pairs={{1,0},{2,1},{3,2},{4,3},{5,4},{6,5},{7,6},{8,7},{9,8},{10,9},{11,1... | collective-permute-start | bytes 13832 | tf_op jit(solution)/shard_map/ppermute | solution.py:296
  31.6 3.3 %copy-start.2 = (f32[4,288]{1,0:T(4,128)}, f32[4,288]{1,0:T(4,128)S(1)}, u32[]{:S(2)}) copy-start(f32[4,288]{1,0:T(4,128)S(1)} %collective-permute-done.before_ref) | copy-start | bytes 13828
  34.9 0.6 %copy-start.3 = (f32[4,288]{1,0:T(4,128)}, f32[4,288]{1,0:T(4,128)S(1)}, u32[]{:S(2)}) copy-start(f32[4,288]{1,0:T(4,128)S(1)} %collective-permute-done.1.after_ref) | copy-start | bytes 13828
  51.7 0.9 %copy-start.1 = (f32[64,288]{1,0:T(8,128)S(1)}, f32[64,288]{1,0:T(8,128)}, u32[]{:S(2)}) copy-start(f32[64,288]{1,0:T(8,128)} %get-tuple-element.4) | copy-start | bytes 221188

commit v2 on v1

v2 whole, which is shorter than its diff:
```python
import functools

import jax
import jax.numpy as jnp
from jax import lax
from jax.experimental import pallas as pl
from jax.experimental.pallas import tpu as pltpu
from jax.sharding import PartitionSpec as P

HALO = 2
LANES = 128
SUBLANES = 8
CHUNK = 32
GROUPS = LANES // CHUNK
core_square = 0.25
softening = 1.5
UNROLL = 4
SPREAD = 8
FOLD = 256
PIECES = 3
VMEM = 32 * 1024 * 1024


def split_rows(width, lanes):
    return pl.cdiv(width, lanes)


def project_kernel(disp_ref, pos_ref, basis_ref, out_ref, stage_scr):
    clusters, rank, width = basis_ref.shape
    spare = LANES - rank
    segments = split_rows(width, spare)
    rows = 2 * HALO
    stage_scr[...] = jnp.zeros_like(stage_scr)

    for side, start in enumerate((0, clusters - HALO)):
        block = jnp.concatenate(
            [disp_ref[start : start + HALO, :], pos_ref[start : start + HALO, :]], axis=0
        )
        for n in range(PIECES):
            piece = block.astype(jnp.bfloat16).astype(jnp.float32)
            block = block - piece
            for g in range(segments):
                size = min(spare, width - g * spare)
                row = side * clusters + (n * segments + g) * rows
                stage_scr[row : row + rows, rank : rank + size] = piece[
                    :, g * spare : g * spare + size
                ]

    disp_bf = disp_ref[...].astype(jnp.bfloat16)
    for k in range(clusters // SUBLANES):
        group = slice(k * SUBLANES, (k + 1) * SUBLANES)
        basis = basis_ref[group].reshape(SUBLANES * rank, width)
        product = lax.dot_general(
            disp_bf[group, :],
            basis,
            (((1,), (1,)), ((), ())),
            preferred_element_type=jnp.float32,
        )
        row = lax.broadcasted_iota(jnp.int32, (SUBLANES, rank), 0)
        coeff = jnp.zeros((SUBLANES, rank), jnp.float32)
        for i in range(SUBLANES):
            coeff = jnp.where(row == i, product[:, i * rank : (i + 1) * rank], coeff)
        stage_scr[group, 0:rank] = coeff
    out_ref[...] = stage_scr[...].astype(out_ref.dtype)


def project(disp, pos, basis):
    clusters, rank, width = basis.shape
    vmem = pl.BlockSpec(memory_space=pltpu.VMEM)
    return pl.pallas_call(
        project_kernel,
        out_shape=jax.ShapeDtypeStruct((2 * clusters, LANES), jnp.bfloat16),
        in_specs=[vmem] * 3,
        out_specs=vmem,
        scratch_shapes=[pltpu.VMEM((2 * clusters, LANES), jnp.float32)],
        compiler_params=pltpu.CompilerParams(vmem_limit_bytes=VMEM),
        cost_estimate=pl.CostEstimate(
            flops=2 * clusters * rank * width,
            bytes_accessed=2 * clusters * rank * width,
            transcendentals=0,
        ),
        name="project",
    )(disp, pos, basis)


def far_kernel(
    count_ref,
    pairs_ref,
    gathered_ref,
    blocks_ref,
    out_ref,
    buffer,
    coeff_scr,
    sum_scr,
    place_scr,
    summed_scr,
    sems,
):
    rank, _, slots = buffer.shape
    cols, clusters, _ = out_ref.shape
    targets = cols * clusters
    rows = gathered_ref.shape[0] // (2 * clusters)
    sources = rows * clusters
    steps = sems.shape[0]
    part = rank // steps

    def fetch(step):
        here = pl.ds(step * part, part)
        return pltpu.make_async_copy(blocks_ref.at[here], buffer.at[here], sems.at[step])

    for step in range(steps):
        fetch(step).start()

    column = jnp.concatenate(
        [gathered_ref[2 * i * clusters : (2 * i + 1) * clusters, :] for i in range(rows)], axis=0
    )
    index = lax.broadcasted_iota(jnp.int32, (sources, slots), 0)
    pick = jnp.where(index == pairs_ref[1:2, :], 1.0, 0.0).astype(jnp.bfloat16)
    coeff = lax.dot_general(
        column, pick, (((0,), (0,)), ((), ())), preferred_element_type=jnp.float32
    )
    coeff_scr[...] = coeff[0:rank, :]

    slot = lax.broadcasted_iota(jnp.int32, (1, slots), 1)
    wanted = jnp.where(slot < count_ref[0], pairs_ref[0:1, :], -1)
    index = lax.broadcasted_iota(jnp.int32, (targets, slots), 0)
    place_scr[...] = jnp.where(index == wanted, 1.0, 0.0).astype(jnp.bfloat16)

    def multiply(step, carry):
        fetch(step).wait()
        for t in range(slots // FOLD):
            lanes = slice(t * FOLD, (t + 1) * FOLD)
            coeff = coeff_scr[:, lanes]
            for r in range(part):
                product = buffer[step * part + r, :, lanes].astype(jnp.float32) * coeff
                folded = product[0:SUBLANES]
                for s in range(1, rank // SUBLANES):
                    folded = folded + product[s * SUBLANES : (s + 1) * SUBLANES]
                start = pl.multiple_of((step * part + r) * SUBLANES, SUBLANES)
                for h in range(FOLD // LANES):
                    sum_scr[t * (FOLD // LANES) + h, pl.ds(start, SUBLANES), :] = folded[
                        :, h * LANES : (h + 1) * LANES
                    ]
        return carry

    lax.fori_loop(0, steps, multiply, 0)

    parts = []
    for t in range(slots // LANES):
        total = sum_scr[t, pl.ds(0, rank, stride=SUBLANES), :]
        for s in range(1, SUBLANES):
            total = total + sum_scr[t, pl.ds(s, rank, stride=SUBLANES), :]
        parts.append(total)
    coupled = jnp.concatenate(parts, axis=1)
    high = coupled.astype(jnp.bfloat16)
    low = (coupled - high.astype(jnp.float32)).astype(jnp.bfloat16)
    both = jnp.concatenate([high, low], axis=0)
    summed = lax.dot_general(
        place_scr[...], both, (((1,), (1,)), ((), ())), preferred_element_type=jnp.float32
    )
    summed_scr[...] = summed + pltpu.roll(summed, rank, 1)

    i = lax.axis_index("rows")
    j = lax.axis_index("cols")
    from_last = jnp.where(j < cols - 1, i, i - 1)
    from_first = jnp.where(j > 0, i, i + 1)
    start = pl.multiple_of((2 * jnp.maximum(from_last, 0) + 1) * clusters, clusters)
    last = gathered_ref[pl.ds(start, clusters), :].astype(jnp.float32)
    last = jnp.where(from_last >= 0, last, 0.0)
    start = pl.multiple_of(2 * jnp.minimum(from_first, rows - 1) * clusters, clusters)
    first = gathered_ref[pl.ds(start, clusters), :].astype(jnp.float32)
    first = jnp.where(from_first < rows, first, 0.0)
    after = jnp.where(j < cols - 1, j + 1, 0)
    lane = lax.broadcasted_iota(jnp.int32, (clusters, LANES), 1)
    for d in range(cols):
        halo = jnp.where(after == d, last, first)
        mine = summed_scr[d * clusters : (d + 1) * clusters, :]
        out_ref[d] = jnp.where(lane < rank, mine, halo).astype(out_ref.dtype)


def far_field(count, pairs, gathered, blocks, cols):
    rank, _, slots = blocks.shape
    rows = lax.axis_size("rows")
    clusters = gathered.shape[0] // (2 * rows)
    steps = SUBLANES
    vmem = pl.BlockSpec(memory_space=pltpu.VMEM)
    smem = pl.BlockSpec(memory_space=pltpu.SMEM)
    return pl.pallas_call(
        far_kernel,
        out_shape=jax.ShapeDtypeStruct((cols, clusters, LANES), jnp.bfloat16),
        in_specs=[smem, vmem, vmem, pl.BlockSpec(memory_space=pl.ANY)],
        out_specs=vmem,
        scratch_shapes=[
            pltpu.VMEM((rank, rank, slots), jnp.bfloat16),
            pltpu.VMEM((rank, slots), jnp.float32),
            pltpu.VMEM((slots // LANES, rank * SUBLANES, LANES), jnp.float32),
            pltpu.VMEM((cols * clusters, slots), jnp.bfloat16),
            pltpu.VMEM((cols * clusters, LANES), jnp.float32),
            pltpu.SemaphoreType.DMA((steps,)),
        ],
        compiler_params=pltpu.CompilerParams(vmem_limit_bytes=VMEM),
        cost_estimate=pl.CostEstimate(
            flops=2 * rank * rank * slots,
            bytes_accessed=2 * rank * rank * slots,
            transcendentals=0,
        ),
        name="far_field",
    )(count, pairs, gathered, blocks)


def traction_kernel(
    pairs_ref,
    count_ref,
    disp_ref,
    pos_ref,
    received_ref,
    intact_ref,
    stiff_ref,
    basis_ref,
    out_ref,
    damage_ref,
    basis_scr,
    ext_scr,
    halo_scr,
    packed_scr,
    src_scr,
    tgt_scr,
    acc_scr,
    sem,
):
    clusters, width = disp_ref.shape
    cols, _, lanes = received_ref.shape
    rank = basis_ref.shape[1]
    elems = width // 3
    chunks = elems // CHUNK
    steps = elems // (GROUPS * SUBLANES)
    spread = elems // GROUPS
    sources = clusters + 2 * HALO
    tiles = ext_scr.shape[2] // LANES
    spare = LANES - rank
    segments = split_rows(width, spare)
    lane = lax.broadcasted_iota(jnp.int32, (SUBLANES, LANES), 1)
    group = lane // CHUNK
    group_start = group * CHUNK

    fetch = pltpu.make_async_copy(basis_ref, basis_scr, sem)
    fetch.start()

    for k, own in enumerate((disp_ref, pos_ref)):
        ext_scr[k, HALO : HALO + clusters, 0:width] = own[...]
    j = lax.axis_index("cols")
    before = jnp.where(j > 0, j - 1, cols - 1)
    after = jnp.where(j < cols - 1, j + 1, 0)
    for start, sender in ((0, before), (HALO + clusters, after)):
        halo_scr[...] = received_ref[sender].astype(jnp.float32)
        size = 2 * HALO * segments
        whole = halo_scr[0:size, :]
        for n in range(1, PIECES):
            whole = whole + halo_scr[n * size : (n + 1) * size, :]
        for g in range(segments):
            count = min(spare, width - g * spare)
            for k in range(2):
                row = (2 * g + k) * HALO
                ext_scr[k, start : start + HALO, g * spare : g * spare + count] = whole[
                    row : row + HALO, rank : rank + count
                ]

    for k in range(2):
        flipped = jnp.concatenate(
            [ext_scr[k, :, t * LANES : (t + 1) * LANES].T for t in range(tiles)], axis=0
        )
        for block in range(packed_scr.shape[0]):
            for c in range(3):
                for f in range(steps):
                    merged = None
                    for g in range(GROUPS):
                        row = c * elems + g * spread + f * SUBLANES
                        piece = flipped[row : row + SUBLANES, :]
                        shift = (g * CHUNK - block * CHUNK) % LANES
                        if shift:
                            piece = pltpu.roll(piece, shift, 1)
                        merged = piece if merged is None else jnp.where(group == g, piece, merged)
                    packed_scr[block, ((1 - k) * 3 + c) * steps + f] = merged

    def spread_sources(it, carry):
        block = it // (CHUNK // SPREAD)
        offset = (it % (CHUNK // SPREAD)) * SPREAD
        for n in range(6 * steps):
            item = packed_scr[block, n]
            for i in range(SPREAD):
                value = jnp.take_along_axis(
                    item, group_start + (offset + i), axis=1, mode="promise_in_bounds"
                )
                src_scr[it * SPREAD + i, n] = value
                if n >= 3 * steps:
                    src_scr[it * SPREAD + i, n + 3 * steps] = 3.0 * value
        return carry

    lax.fori_loop(0, pl.cdiv(sources, SPREAD), spread_sources, 0)

    within = lax.broadcasted_iota(jnp.int32, (clusters, LANES), 1) % CHUNK
    for m in range(3 * chunks):
        tile = m // GROUPS
        own = ext_scr[1, HALO : HALO + clusters, tile * LANES : (tile + 1) * LANES]
        tgt_scr[:, m, :] = jnp.take_along_axis(
            own, within + (m % GROUPS) * CHUNK, axis=1, mode="promise_in_bounds"
        )

    acc_scr[...] = jnp.zeros_like(acc_scr)
    count = count_ref[0]

    def one_pair(slot):
        target = pairs_ref[0, slot]
        source = pairs_ref[1, slot]
        into = jnp.where(slot < count, target, clusters) * SUBLANES
        into = pl.multiple_of(into, SUBLANES)
        tgt = [
            jnp.broadcast_to(tgt_scr[target, m : m + 1, :], (SUBLANES, LANES))
            for m in range(3 * chunks)
        ]
        sums = [None] * (3 * chunks)
        for f in range(steps):
            y = [src_scr[source, c * steps + f] for c in range(3)]
            u = [src_scr[source, (3 + c) * steps + f] for c in range(3)]
            v = [src_scr[source, (6 + c) * steps + f] for c in range(3)]
            for h in range(chunks):
                r = [tgt[c * chunks + h] - y[c] for c in range(3)]
                q = (r[0] * r[0] + core_square) + (r[1] * r[1] + r[2] * r[2])
                s = r[0] * v[0] + (r[1] * v[1] + r[2] * v[2])
                inverse = lax.rsqrt(q)
                square = inverse * inverse
                weight = square * inverse
                s = s * square
                for c in range(3):
                    term = weight * (u[c] - s * r[c])
                    m = c * chunks + h
                    sums[m] = term if sums[m] is None else sums[m] + term
        for m in range(3 * chunks):
            acc_scr[m, pl.ds(into, SUBLANES), :] += sums[m]

    def step(it, carry):
        for k in range(UNROLL):
            one_pair(it * UNROLL + k)
        return carry

    lax.fori_loop(0, (count + UNROLL - 1) // UNROLL, step, 0)

    owned = received_ref[0].astype(jnp.float32)
    for d in range(1, cols):
        owned = owned + received_ref[d].astype(jnp.float32)
    fetch.wait()
    wide = lax.broadcasted_iota(jnp.int32, (SUBLANES, SUBLANES * rank), 1) // rank
    wide = wide == lax.broadcasted_iota(jnp.int32, (SUBLANES, SUBLANES * rank), 0)
    for k in range(clusters // SUBLANES):
        some = slice(k * SUBLANES, (k + 1) * SUBLANES)
        tiled = jnp.concatenate([owned[some, 0:rank]] * SUBLANES, axis=1)
        diagonal = jnp.where(wide, tiled, 0.0).astype(jnp.bfloat16)
        ext_scr[1, some, 0:width] = jnp.dot(
            diagonal,
            basis_scr[some].reshape(SUBLANES * rank, width),
            preferred_element_type=jnp.float32,
        )

    own_group = lax.broadcasted_iota(jnp.int32, (clusters, LANES), 1) // CHUNK
    for t in range(tiles):
        merged = None
        for g in range(GROUPS):
            m = t * GROUPS + g
            if m >= 3 * chunks:
                break
            total = acc_scr[m, pl.ds(0, clusters, stride=SUBLANES), :]
            for s in range(1, SUBLANES):
                total = total + acc_scr[m, pl.ds(s, clusters, stride=SUBLANES), :]
            total = total + pltpu.roll(total, 2 * CHUNK, 1)
            total = total + pltpu.roll(total, CHUNK, 1)
            merged = total if merged is None else jnp.where(own_group == g, total, merged)
        ext_scr[0, 0:clusters, t * LANES : (t + 1) * LANES] = merged

    disp = [disp_ref[:, c * elems : (c + 1) * elems] for c in range(3)]
    separation = jnp.sqrt(1.0 + (disp[0] * disp[0] + disp[1] * disp[1] + disp[2] * disp[2]))
    softened = 1.0 - jnp.exp(-(separation - 1.0) / softening)
    intact = intact_ref[...].astype(jnp.float32)
    damage = intact * softened + (1.0 - intact)
    damage_ref[...] = damage
    hold = (1.0 - damage) * stiff_ref[...]
    for c in range(3):
        here = slice(c * elems, (c + 1) * elems)
        elastic = ext_scr[0, 0:clusters, here] + ext_scr[1, 0:clusters, here]
        out_ref[:, here] = elastic - hold * disp[c]


def traction_field(pairs, count, disp, pos, received, intact, stiffness, basis):
    clusters, width = disp.shape
    rank = basis.shape[1]
    elems = width // 3
    chunks = elems // CHUNK
    steps = elems // (GROUPS * SUBLANES)
    sources = clusters + 2 * HALO
    padded = pl.cdiv(width, LANES) * LANES
    slots = pairs.shape[1]
    vmem = pl.BlockSpec(memory_space=pltpu.VMEM)
    smem = pl.BlockSpec(memory_space=pltpu.SMEM)
    return pl.pallas_call(
        traction_kernel,
        out_shape=(
            jax.ShapeDtypeStruct((clusters, width), jnp.float32),
            jax.ShapeDtypeStruct((clusters, elems), jnp.float32),
        ),
        in_specs=[smem, smem] + [vmem] * 5 + [pl.BlockSpec(memory_space=pl.ANY)],
        out_specs=(vmem, vmem),
        scratch_shapes=[
            pltpu.VMEM(basis.shape, basis.dtype),
            pltpu.VMEM((2, LANES, padded), jnp.float32),
            pltpu.VMEM((clusters, LANES), jnp.float32),
            pltpu.VMEM((pl.cdiv(sources, CHUNK), 6 * steps, SUBLANES, LANES), jnp.float32),
            pltpu.VMEM(
                (pl.cdiv(sources, SPREAD) * SPREAD, 9 * steps, SUBLANES, LANES), jnp.float32
            ),
            pltpu.VMEM((clusters, 3 * chunks, LANES), jnp.float32),
            pltpu.VMEM((3 * chunks, (clusters + 1) * SUBLANES, LANES), jnp.float32),
            pltpu.SemaphoreType.DMA(()),
        ],
        compiler_params=pltpu.CompilerParams(vmem_limit_bytes=VMEM),
        cost_estimate=pl.CostEstimate(
            flops=30 * slots * elems * elems,
            bytes_accessed=4 * clusters * width * 6 + 2 * clusters * rank * width,
            transcendentals=slots * elems * elems,
        ),
        name="traction",
    )(pairs, count, disp, pos, received, intact, stiffness, basis)


def local(
    displacement,
    positions,
    cluster_basis,
    near_pairs,
    near_count,
    far_pairs,
    far_count,
    far_blocks,
    intact,
    stiffness,
):
    cols = lax.axis_size("cols")
    basis = cluster_basis.transpose(0, 2, 1)
    payload = project(displacement, positions, basis)
    gathered = lax.all_gather(payload, "rows", axis=0, tiled=True)
    partial = far_field(far_count, far_pairs.T, gathered, far_blocks.transpose(1, 2, 0), cols)
    received = lax.all_to_all(partial, "cols", split_axis=0, concat_axis=0)
    return traction_field(
        near_pairs.T, near_count, displacement, positions, received, intact, stiffness, basis
    )


def solution(mesh):
    both = ("rows", "cols")
    in_specs = (
        P(both, None),
        P(both, None),
        P(both, None, None),
        P(both, None),
        P(both),
        P(both, None),
        P(both),
        P(both, None, None),
        P(both, None),
        P(both, None),
    )
    out_specs = (P(both, None), P(both, None))
    return jax.shard_map(local, mesh=mesh, in_specs=in_specs, out_specs=out_specs, check_vma=False)
```

time: 53.8 us -> 49.6 us (0.922)
  the two profiles are of different devices: /device:TPU:22 before, /device:TPU:0 now
where the time goes in v2:
time: 49.6 us; the launch traced here: 49.2 us
  Pallas kernels  19.9 us (40%)
  local copies, waits for them, and re-layouts  7.76 us (16%)
  waiting for transfers between devices  6.84 us (14%)
  blocking collectives  6.5 us (13%)
  starting transfers between devices  6.19 us (12%)
  between operations  2.01 us (4%)
    pallas_call x1, Pallas kernels, traction_field(): pl.pallas_call(traction_kernel, out_shape=(jax.ShapeDtypeStruct((clusters...  14.3 us
    unnamed x22, local copies, waits for them, and re-layouts  7.76 us
    all_to_all x1, waiting for transfers between devices, local(): received = lax.all_to_all(partial, 'cols', split_axis=0, concat_axis=0)  6.84 us
    all_gather x1, blocking collectives, local(): gathered = lax.all_gather(payload, 'rows', axis=0, tiled=True)  6.5 us
    all_to_all x1, starting transfers between devices, local(): received = lax.all_to_all(partial, 'cols', split_axis=0, concat_axis=0)  6.19 us
    pallas_call x1, Pallas kernels, far_field(): pl.pallas_call(far_kernel, out_shape=jax.ShapeDtypeStruct((cols, clusters...  4.15 us
    pallas_call x1, Pallas kernels, project(): pl.pallas_call(project_kernel, out_shape=jax.ShapeDtypeStruct((2 * cluste...  1.47 us
  transfers between devices with their start and end apart: 1, of which 1 were waited for; matrix products, arithmetic and copies ran while one was open for 0% of the time, Pallas kernels for 0%

profile of v2, /device:TPU:0, one launch (start us, length us, event | category | flops | bytes accessed | tf_op | source)
XLA Modules:
  0.0 49.2 jit_solution(11849762328837963783)
XLA Ops:
  0.6 0.0 copy-start.1
  0.6 1.9 %copy-done.1 = bf16[64,288,64]{1,2,0:T(8,128)(2,1)S(1)} copy-done((bf16[64,288,64]{1,2,0:T(8,128)(2,1)S(1)}, bf16[64,288,64]{1,2,0:T(8,128)(2,1)}, u32[]{:S(2)}) %copy-start.1) | copy-done | bytes 2359320
  2.5 0.0 copy-start.3
  2.5 0.9 %copy-done.3 = f32[64,288]{1,0:T(8,128)S(1)} copy-done((f32[64,288]{1,0:T(8,128)S(1)}, f32[64,288]{1,0:T(8,128)}, u32[]{:S(2)}) %copy-start.3) | copy-done | bytes 73752
  3.4 0.0 copy-start.5
  3.4 0.9 %copy-done.5 = f32[64,288]{1,0:T(8,128)S(1)} copy-done((f32[64,288]{1,0:T(8,128)S(1)}, f32[64,288]{1,0:T(8,128)}, u32[]{:S(2)}) %copy-start.5) | copy-done | bytes 73752
  4.3 0.0 copy-start.2
  4.3 0.0 copy-start.4
  4.3 0.0 copy-start.6
  4.3 0.0 copy-start.8
  4.3 0.0 copy-start.9
  4.3 0.0 copy-start.10
  4.3 1.5 %project.1 = bf16[128,128]{1,0:T(8,128)(2,1)S(1)} custom-call(f32[64,288]{1,0:T(8,128)S(1)} %copy-done.3, f32[64,288]{1,0:T(8,128)S(1)} %copy-done.5, bf16[64,64,288]{2,1,0:T(8,128)(2,1)S(1)} %bitcast.5), custom_call_target="tpu_custom_call" | custom-call | flops 2359296 | bytes 2359296 | tf_op jit(solution)/shard_map/project/pallas_call | solution.py:70
  5.8 6.5 %all_gather.3.gathered_ref = bf16[512,128]{1,0:T(8,128)(2,1)S(1)} all-gather(bf16[128,128]{1,0:T(8,128)(2,1)S(1)} %project.1), channel_id=1, replica_groups=mesh['rows'=4,'cols'=8] {'rows'}, dimensions={0}, use_global_device_ids=true | all-gather | bytes 163840 | tf_op jit(solution)/shard_map/all_gather | solution.py:448
  13.0 0.0 copy-start
  13.0 3.4 %copy-done = bf16[1024,64,64]{0,2,1:T(8,128)(2,1)S(1)} copy-done((bf16[1024,64,64]{0,2,1:T(8,128)(2,1)S(1)}, bf16[1024,64,64]{0,2,1:T(8,128)(2,1)}, u32[]{:S(2)}) %copy-start) | copy-done | bytes 8388632
  16.3 0.0 copy-start.7
  16.4 0.7 %copy-done.7 = s32[1024,2]{0,1:T(2,128)S(1)} copy-done((s32[1024,2]{0,1:T(2,128)S(1)}, s32[1024,2]{0,1:T(2,128)}, u32[]{:S(2)}) %copy-start.7) | copy-done | bytes 8216
  17.0 4.2 %far_field.1 = bf16[8,64,128]{2,1,0:T(8,128)(2,1)} custom-call(s32[1]{0:T(128)S(6)} %copy.13.count_ref, s32[2,1024]{1,0:T(2,128)S(1)} %bitcast.7, bf16[512,128]{1,0:T(8,128)(2,1)S(1)} %all_gather.3.gathered_ref, bf16[64,64,1024]{2,1,0:T(8,128)(2,1)S(1)} %bitcast.4), custom_call_target="tpu_custom_call" | custom-call | flops 8388608 | bytes 8388608 | tf_op jit(solution)/shard_map/far_field/pallas_call | solution.py:188
  21.2 6.2 %all-to-all-start = ((bf16[8,64,128]{2,1,0:T(8,128)(2,1)}), bf16[8,64,128]{2,1,0:T(8,128)(2,1)S(1)}, u32[]{:S(2)}, u32[]{:S(2)}) async-start(bf16[8,64,128]{2,1,0:T(8,128)(2,1)} %far_field.1), calls=%async_computation | async-start | bytes 262144 | tf_op jit(solution)/shard_map/all_to_all | solution.py:450
  28.0 6.8 %all-to-all-done.received_ref = bf16[8,64,128]{2,1,0:T(8,128)(2,1)S(1)} async-done(((bf16[8,64,128]{2,1,0:T(8,128)(2,1)}), bf16[8,64,128]{2,1,0:T(8,128)(2,1)S(1)}, u32[]{:S(2)}, u32[]{:S(2)}) %all-to-all-start) | async-done | bytes 131104 | tf_op jit(solution)/shard_map/all_to_all | solution.py:450
  34.9 0.0 copy-done.2
  34.9 0.0 copy-done.4
  34.9 0.0 copy-done.6
  34.9 0.0 copy-done.8
  34.9 0.0 copy-done.9
  34.9 0.0 copy-done.10
  34.9 14.3 %traction.1 = (f32[64,288]{1,0:T(8,128)}, f32[64,96]{1,0:T(8,128)}) custom-call(s32[2,256]{1,0:T(2,128)S(1)} %bitcast.8, s32[1]{0:T(128)S(6)} %copy.12.count_ref, f32[64,288]{1,0:T(8,128)S(1)} %copy-done.4, f32[64,288]{1,0:T(8,128)S(1)} %copy-done.6, bf16[8,64,128]{2,1,0:T(8,128)(2,1)S(1)} %all-to-all-done.received_ref, s32[64,96]{1,0:T(8,128)S(1)} %copy-done.8, ...), custom_call_target="tpu_custom_call" | custom-call | flops 70778880 | bytes 2801664 | tf_op jit(solution)/shard_map/traction/pallas_call | solution.py:403
Async XLA Ops:
  0.6 1.9 %copy-start.1 = (bf16[64,288,64]{1,2,0:T(8,128)(2,1)S(1)}, bf16[64,288,64]{1,2,0:T(8,128)(2,1)}, u32[]{:S(2)}) copy-start(bf16[64,288,64]{1,2,0:T(8,128)(2,1)} %param.12) | copy-start | bytes 7077892
  2.5 0.9 %copy-start.3 = (f32[64,288]{1,0:T(8,128)S(1)}, f32[64,288]{1,0:T(8,128)}, u32[]{:S(2)}) copy-start(f32[64,288]{1,0:T(8,128)} %disp_ref.3) | copy-start | bytes 221188
  3.4 0.9 %copy-start.5 = (f32[64,288]{1,0:T(8,128)S(1)}, f32[64,288]{1,0:T(8,128)}, u32[]{:S(2)}) copy-start(f32[64,288]{1,0:T(8,128)} %pos_ref.3) | copy-start | bytes 221188
  4.3 30.6 %copy-start.2 = (bf16[64,288,64]{1,2,0:T(8,128)(2,1)S(1)}, bf16[64,288,64]{1,2,0:T(8,128)(2,1)}, u32[]{:S(2)}) copy-start(bf16[64,288,64]{1,2,0:T(8,128)(2,1)} %param.12) | copy-start | bytes 7077892
  4.3 30.6 %copy-start.4 = (f32[64,288]{1,0:T(8,128)S(1)}, f32[64,288]{1,0:T(8,128)}, u32[]{:S(2)}) copy-start(f32[64,288]{1,0:T(8,128)} %disp_ref.3) | copy-start | bytes 221188
  4.3 30.6 %copy-start.6 = (f32[64,288]{1,0:T(8,128)S(1)}, f32[64,288]{1,0:T(8,128)}, u32[]{:S(2)}) copy-start(f32[64,288]{1,0:T(8,128)} %pos_ref.3) | copy-start | bytes 221188
  4.3 30.6 %copy-start.8 = (s32[64,96]{1,0:T(8,128)S(1)}, s32[64,96]{1,0:T(8,128)}, u32[]{:S(2)}) copy-start(s32[64,96]{1,0:T(8,128)} %intact_ref.1) | copy-start | bytes 73732
  4.3 30.6 %copy-start.9 = (f32[64,96]{1,0:T(8,128)S(1)}, f32[64,96]{1,0:T(8,128)}, u32[]{:S(2)}) copy-start(f32[64,96]{1,0:T(8,128)} %stiff_ref.1) | copy-start | bytes 73732
  4.3 30.6 %copy-start.10 = (s32[256,2]{0,1:T(2,128)S(1)}, s32[256,2]{0,1:T(2,128)}, u32[]{:S(2)}) copy-start(s32[256,2]{0,1:T(2,128)} %param.13) | copy-start | bytes 6148
  13.0 3.4 %copy-start = (bf16[1024,64,64]{0,2,1:T(8,128)(2,1)S(1)}, bf16[1024,64,64]{0,2,1:T(8,128)(2,1)}, u32[]{:S(2)}) copy-start(bf16[1024,64,64]{0,2,1:T(8,128)(2,1)} %param.17) | copy-start | bytes 25165828
  16.3 0.7 %copy-start.7 = (s32[1024,2]{0,1:T(2,128)S(1)}, s32[1024,2]{0,1:T(2,128)}, u32[]{:S(2)}) copy-start(s32[1024,2]{0,1:T(2,128)} %param.15) | copy-start | bytes 24580
  21.2 13.7 %all-to-all-start = ((bf16[8,64,128]{2,1,0:T(8,128)(2,1)}), bf16[8,64,128]{2,1,0:T(8,128)(2,1)S(1)}, u32[]{:S(2)}, u32[]{:S(2)}) async-start(bf16[8,64,128]{2,1,0:T(8,128)(2,1)} %far_field.1), calls=%async_computation | async-start | bytes 262144 | tf_op jit(solution)/shard_map/all_to_all | solution.py:450
